TPU v7x, 256 devices: a whole 4x4x8 slice. The times are simulated.
256 devices in a mesh: batch: 4 (over y_lo, core), feat: 64 (over z, x, y_hi).
Axes of the slice: x: 4, y: 4 (y_hi: 2, y_lo: 2; y = y_hi * 2 + y_lo), z: 8, core: 2. Of those that a mesh axis runs over, the one named last changes fastest.
Arguments:
- embedding: bfloat16 [512, 16384], P('batch', 'feat'), may hold values from -16 to 16
Outputs:
- embedding_grad: bfloat16 [512, 16384], P('batch', 'feat')
- cov_tiles: bfloat16 [192, 1024, 1024], P('feat', 'batch')
All inputs are finite; a program needn't handle non-finite values.
Results may differ from a plain program's by a relative error of at most 0.0056.
Values may be sent and summed in bfloat16 or wider, within the bound.
No kernel may reach another device: no remote copies, remote signals or barrier semaphores. Data moves between devices by JAX's collectives and lax.ppermute only.
A program may use at most 128 MiB of HBM per device.

v0:
```python
import collections

import jax
import jax.numpy as jnp
import numpy as np
from jax import lax
from jax.experimental import pallas as pl
from jax.experimental.pallas import tpu as pltpu
from jax.sharding import Mesh
from jax.sharding import PartitionSpec as P

BLK = 1024
NBLK = 16
TILES = 136
FEATS = 64
PIECE = 256
SLOTS = 3
ENTRIES = 16
BATCH = ("yl", "co")
FEAT = ("z", "x", "yh")
EVERY = BATCH + FEAT


def tiles_of(f):
    upper_rows, upper_cols = np.triu_indices(NBLK)
    ids = range(f, TILES, FEATS)
    return [(int(upper_rows[t]), int(upper_cols[t])) for t in ids]


def blocks_of(f):
    found = []
    for pair in tiles_of(f):
        for j in pair:
            if j not in found:
                found.append(j)
    return found


def edge_rounds(edges):
    degree = collections.Counter()
    for s, d in edges:
        degree[("s", s)] += 1
        degree[("d", d)] += 1
    count = max(degree.values())
    taken = collections.defaultdict(dict)
    for s, d in edges:
        u, v = ("s", s), ("d", d)
        a = next(c for c in range(count) if c not in taken[u])
        b = next(c for c in range(count) if c not in taken[v])
        if a != b:
            path, node, c = [], v, a
            while c in taken[node]:
                other = taken[node][c]
                path.append((node, other, c))
                node, c = other, (b if c == a else a)
            for p, q, c in path:
                del taken[p][c]
                del taken[q][c]
            for p, q, c in path:
                o = b if c == a else a
                taken[p][o] = q
                taken[q][o] = p
        taken[u][a] = v
        taken[v][a] = u
    rounds = [[] for _ in range(count)]
    for u, row in taken.items():
        if u[0] == "s":
            for c, v in row.items():
                rounds[c].append((u[1], v[1]))
    return [sorted(r) for r in rounds]


def make_plan():
    used = collections.Counter()
    edges = []
    for f in range(FEATS):
        for j in blocks_of(f):
            for q in range(4):
                p = 4 * j + q
                if p == f:
                    continue
                y_half = q // 2
                source_half = y_half if p % 2 == f % 2 else 1 - y_half
                free = [used[(p, source_half, c)] for c in range(2)]
                core = 0 if free[0] < free[1] or (free[0] == free[1] and f % 2) else 1
                used[(p, source_half, core)] += 1
                edges.append(((source_half * 2 + core) * FEATS + p, q * FEATS + f))
    rounds = edge_rounds(edges)
    place = {}
    for r, pairs in enumerate(rounds):
        for s, d in pairs:
            place[(d, s % FEATS)] = r
    table = np.full((4, FEATS, ENTRIES), -1, np.int32)
    for f in range(FEATS):
        for q in range(4):
            for k, pair in enumerate(tiles_of(f)):
                for side, j in enumerate(pair):
                    p = 4 * j + q
                    table[q, f, 2 * k + side] = len(rounds) if p == f else place[(q * FEATS + f, p)]
                table[q, f, 2 * SLOTS + k] = int(pair[0] == pair[1])
    return rounds, table.reshape(-1)


def my_entries(table_ref):
    index = ((lax.axis_index("yl") * 2 + lax.axis_index("co")) * 8 + lax.axis_index("z")) * 8
    index = index + lax.axis_index("x") * 2 + lax.axis_index("yh")
    return [table_ref[index * ENTRIES + i] for i in range(3 * SLOTS)]


def fetch(entry, sources, target, sem):
    for r, source in enumerate(sources):

        @pl.when(entry == r)
        def _():
            pltpu.make_async_copy(source, target, sem).start()


def fetched(entry, source, target, sem):
    @pl.when(entry >= 0)
    def _():
        pltpu.make_async_copy(source, target, sem).wait()


def pick_kernel(table_ref, *refs):
    sources, (right_ref, last_ref, sems) = refs[:-3], refs[-3:]
    entry = my_entries(table_ref)
    targets = [right_ref.at[0], right_ref.at[1], last_ref]
    for k in range(SLOTS):
        fetch(entry[2 * k + 1], sources, targets[k], sems.at[k])
    for k in range(SLOTS):
        fetched(entry[2 * k + 1], sources[0], targets[k], sems.at[k])


def tile_kernel(scale, table_ref, *refs):
    sources, rights, lasts = refs[:-11], refs[-11:-7], refs[-7:-3]
    out_ref, left_ref, sems = refs[-3:]
    yl, co = lax.axis_index("yl"), lax.axis_index("co")
    entry = my_entries(table_ref)
    for k in range(SLOTS):
        fetch(entry[2 * k], sources, left_ref.at[k], sems.at[k])
    for k in range(SLOTS):
        fetched(entry[2 * k], sources[0], left_ref.at[k], sems.at[k])

    def fill(k, pieces):
        left = left_ref[k].T
        for n, piece in enumerate(pieces):
            q = (yl ^ (n // 2)) * 2 + (co ^ (n % 2))
            cols = pl.ds(pl.multiple_of(q * PIECE, PIECE), PIECE)
            cov = jnp.dot(left, piece[...], preferred_element_type=jnp.float32) / scale
            on_diagonal = lax.broadcasted_iota(jnp.int32, cov.shape, 0) == lax.broadcasted_iota(
                jnp.int32, cov.shape, 1
            )
            dropped = on_diagonal & (entry[2 * SLOTS + k] == 1) & (n == 0)
            out_ref[k, :, cols] = jnp.where(dropped, 0.0, cov).astype(out_ref.dtype)

    for k in range(2):
        fill(k, [piece.at[k] for piece in rights])

    @pl.when(entry[4] >= 0)
    def _():
        fill(2, lasts)

    @pl.when(entry[4] < 0)
    def _():
        out_ref[2] = jnp.zeros(out_ref.shape[1:], out_ref.dtype)


def shards(embedding):
    local_rows, local_cols = embedding.shape
    rounds, table = make_plan()
    table = jnp.asarray(table)
    row_count = 4 * local_rows
    b = lax.axis_index(BATCH)
    values = lax.all_gather(embedding, BATCH, axis=0, tiled=True).astype(jnp.float32)
    col_mean = jnp.sum(values, axis=0) / row_count
    deviation = values - col_mean
    col_std = jnp.sqrt(jnp.sum(deviation * deviation, axis=0) / (row_count - 1) + 0.0001)
    exact = lax.reduce_precision(deviation, 8, 7)
    centered = exact.astype(jnp.bfloat16)
    arrived = [lax.ppermute(centered, EVERY, pairs) for pairs in rounds]

    my_values = embedding.astype(jnp.float32)
    my_deviation = my_values - col_mean
    var_grad = jnp.where(col_std < 1.0, -6.25 * my_deviation / col_std, 0.0)
    my_exact = lax.reduce_precision(my_deviation, 8, 7)
    gram = lax.dot_general(
        my_exact.astype(jnp.bfloat16), centered, (((1,), (1,)), ((), ())), preferred_element_type=jnp.float32
    )
    part = lax.all_to_all(gram.reshape(8, -1, row_count), "z", 0, 0).sum(0)
    part = lax.all_to_all(jnp.broadcast_to(part, (8, *part.shape)), ("x", "yh"), 0, 0).sum(0)
    gram = lax.all_to_all(jnp.broadcast_to(part, (8, *part.shape)), "z", 0, 0).reshape(local_rows, row_count)
    gram_hi = lax.reduce_precision(gram, 8, 7)
    gram_lo = (gram - gram_hi).astype(jnp.bfloat16)
    whole = jnp.dot(gram_hi.astype(jnp.bfloat16), centered, preferred_element_type=jnp.float32)
    whole = whole + jnp.dot(gram_lo, centered, preferred_element_type=jnp.float32)
    diagonal = jnp.sum(exact * exact, axis=0)
    cov_grad = (whole - my_exact * diagonal) / (row_count - 1)
    grad = (cov_grad + var_grad).astype(jnp.bfloat16)

    sources = [*arrived, centered]
    anywhere = pl.BlockSpec(memory_space=pl.ANY)
    vmem = pl.BlockSpec(memory_space=pltpu.VMEM)
    smem = pl.BlockSpec(memory_space=pltpu.SMEM)
    right, last = pl.pallas_call(
        pick_kernel,
        out_shape=(
            jax.ShapeDtypeStruct((2, row_count, PIECE), jnp.bfloat16),
            jax.ShapeDtypeStruct((row_count, PIECE), jnp.bfloat16),
        ),
        in_specs=[smem] + [anywhere] * len(sources),
        out_specs=(vmem, vmem),
        scratch_shapes=[pltpu.SemaphoreType.DMA((SLOTS,))],
        compiler_params=pltpu.CompilerParams(vmem_limit_bytes=16 * 2**20),
    )(table, *sources)
    swap = [(0, 1), (1, 0)]
    swap_first = [(0, 8), (8, 0)]
    right_y = lax.ppermute(right, "yl", swap)
    right_c = lax.ppermute(right, "co", swap)
    right_yc = lax.ppermute(right_y, "co", swap)
    last_y = lax.ppermute(last, ("yl", "z"), swap_first)
    last_c = lax.ppermute(last, ("co", "z"), swap_first)
    last_yc = lax.ppermute(last_y, ("co", "z"), swap_first)
    tiles = pl.pallas_call(
        lambda *refs: tile_kernel(row_count - 1, *refs),
        out_shape=jax.ShapeDtypeStruct((SLOTS, PIECE, BLK), jnp.bfloat16),
        in_specs=[smem] + [anywhere] * len(sources) + [vmem] * 8,
        out_specs=vmem,
        scratch_shapes=[
            pltpu.VMEM((SLOTS, row_count, PIECE), jnp.bfloat16),
            pltpu.SemaphoreType.DMA((SLOTS,)),
        ],
        compiler_params=pltpu.CompilerParams(vmem_limit_bytes=32 * 2**20),
    )(table, *sources, right, right_c, right_y, right_yc, last, last_c, last_y, last_yc)
    return grad, tiles


def solution(mesh):
    split = Mesh(mesh.devices.reshape(2, 2, 8, 4, 2), EVERY)
    in_specs = (P(BATCH, FEAT),)
    out_specs = (P(BATCH, FEAT), P(FEAT, BATCH, None))
    return jax.shard_map(shards, mesh=split, in_specs=in_specs, out_specs=out_specs, check_vma=False)
```

profile of v0, /device:TPU:1, one launch (start us, length us, event | category | flops | bytes accessed | tf_op | source)
XLA Modules:
  0.0 97.4 jit_solution(4619283845256475083)
XLA Ops:
  0.6 9.1 %all_gather.3 = bf16[512,256]{1,0:T(8,128)(2,1)S(1)} all-gather(bf16[128,256]{1,0:T(8,128)(2,1)} %param.2), channel_id=1, replica_groups=mesh['yl'=2,'co'=2,'z'=8,'x'=4,'yh'=2] {'yl','co'}, dimensions={0}, use_global_device_ids=true | all-gather | bytes 327680 | tf_op jit(solution)/shard_map/all_gather | solution.py:174
  9.9 1.8 %fusion.13 = f32[128,512]{1,0:T(8,128)} fusion(bf16[512,256]{1,0:T(8,128)(2,1)S(1)} %get-tuple-element.8.refs_6_.refs_7_, bf16[128,256]{1,0:T(8,128)(2,1)} %param.2, f32[256]{0:T(256)S(1)} %broadcast_multiply_fusion), kind=kOutput, calls=%fused_computation.19 | convolution fusion | flops 33685504 | bytes 590848 | tf_op jit(solution)/shard_map/dot_general | solution.py:186
  11.7 6.5 %all-to-all-start = ((f32[8,16,512]{2,1,0:T(8,128)}), f32[8,16,512]{2,1,0:T(8,128)S(1)}, u32[]{:S(2)}, u32[]{:S(2)}) async-start(f32[8,16,512]{2,1,0:T(8,128)} %bitcast), calls=%async_computation | async-start | bytes 524288 | tf_op jit(solution)/shard_map/all_to_all | solution.py:189
  18.2 4.9 %collective-permute-start = (bf16[512,256]{1,0:T(8,128)(2,1)S(1)}, bf16[512,256]{1,0:T(8,128)(2,1)S(1)}, u32[]{:S(2)}, u32[]{:S(2)}) collective-permute-start(bf16[512,256]{1,0:T(8,128)(2,1)S(1)} %get-tuple-element.8.refs_6_.refs_7_), channel_id=1, source_target_pairs={{0,4},{1,75},{2,133},{3,206},{4,30},{5,65},{6,155},{7,218},{8,36},... | collective-permute-start | bytes 786440 | tf_op jit(solution)/shard_map/ppermute | solution.py:180
  23.1 8.8 %collective-permute-start.1 = (bf16[512,256]{1,0:T(8,128)(2,1)S(1)}, bf16[512,256]{1,0:T(8,128)(2,1)S(1)}, u32[]{:S(2)}, u32[]{:S(2)}) collective-permute-start(bf16[512,256]{1,0:T(8,128)(2,1)S(1)} %get-tuple-element.8.refs_6_.refs_7_), channel_id=1, source_target_pairs={{0,8},{1,67},{2,141},{3,194},{4,26},{5,83},{6,151},{7,214},{8,32},... | collective-permute-start | bytes 786440 | tf_op jit(solution)/shard_map/ppermute | solution.py:180
  31.9 1.9 %collective-permute-start.2 = (bf16[512,256]{1,0:T(8,128)(2,1)S(1)}, bf16[512,256]{1,0:T(8,128)(2,1)S(1)}, u32[]{:S(2)}, u32[]{:S(2)}) collective-permute-start(bf16[512,256]{1,0:T(8,128)(2,1)S(1)} %get-tuple-element.8.refs_6_.refs_7_), channel_id=1, source_target_pairs={{0,12},{1,79},{2,137},{3,198},{4,18},{5,91},{6,129},{7,222},{8,40}... | collective-permute-start | bytes 786440 | tf_op jit(solution)/shard_map/ppermute | solution.py:180
  33.8 4.6 %collective-permute-start.3 = (bf16[512,256]{1,0:T(8,128)(2,1)S(1)}, bf16[512,256]{1,0:T(8,128)(2,1)S(1)}, u32[]{:S(2)}, u32[]{:S(2)}) collective-permute-start(bf16[512,256]{1,0:T(8,128)(2,1)S(1)} %get-tuple-element.8.refs_6_.refs_7_), channel_id=1, source_target_pairs={{2,129},{3,202},{4,22},{5,87},{6,147},{7,210},{8,44},{9,105},{10,1... | collective-permute-start | bytes 786440 | tf_op jit(solution)/shard_map/ppermute | solution.py:180
  38.4 1.3 %collective-permute-start.4 = (bf16[512,256]{1,0:T(8,128)(2,1)S(1)}, bf16[512,256]{1,0:T(8,128)(2,1)S(1)}, u32[]{:S(2)}, u32[]{:S(2)}) collective-permute-start(bf16[512,256]{1,0:T(8,128)(2,1)S(1)} %get-tuple-element.8.refs_6_.refs_7_), channel_id=1, source_target_pairs={{1,71},{26,135},{46,129},{48,2},{49,65},{51,194},{52,4},{53,67},{5... | collective-permute-start | bytes 786440 | tf_op jit(solution)/shard_map/ppermute | solution.py:180
  39.8 0.7 collective-permute-start.5
  40.5 0.7 broadcast_in_dim.18
  41.2 5.6 %all-to-all-start.1 = ((f32[8,16,512]{2,1,0:T(8,128)}), f32[8,16,512]{2,1,0:T(8,128)S(1)}, u32[]{:S(2)}, u32[]{:S(2)}) async-start(f32[8,16,512]{2,1,0:T(8,128)} %broadcast_in_dim.18), calls=%async_computation.1 | async-start | bytes 524288 | tf_op jit(solution)/shard_map/all_to_all | solution.py:190
  46.9 3.0 %collective-permute-done.2.refs_2_.refs_3_ = bf16[512,256]{1,0:T(8,128)(2,1)S(1)} collective-permute-done((bf16[512,256]{1,0:T(8,128)(2,1)S(1)}, bf16[512,256]{1,0:T(8,128)(2,1)S(1)}, u32[]{:S(2)}, u32[]{:S(2)}) %collective-permute-start.2) | collective-permute-done | bytes 262176 | tf_op jit(solution)/shard_map/ppermute | solution.py:180
  49.9 3.2 %collective-permute-done.4.refs_4_.refs_5_ = bf16[512,256]{1,0:T(8,128)(2,1)S(1)} collective-permute-done((bf16[512,256]{1,0:T(8,128)(2,1)S(1)}, bf16[512,256]{1,0:T(8,128)(2,1)S(1)}, u32[]{:S(2)}, u32[]{:S(2)}) %collective-permute-start.4) | collective-permute-done | bytes 262176 | tf_op jit(solution)/shard_map/ppermute | solution.py:180
  53.1 1.7 %shard_map.41 = (bf16[2,512,256]{2,1,0:T(8,128)(2,1)S(1)}, bf16[512,256]{1,0:T(8,128)(2,1)}) custom-call(s32[4096]{0:T(1024)S(1)} %copy-done, bf16[512,256]{1,0:T(8,128)(2,1)S(1)} %collective-permute-done.refs_0_.refs_1_, bf16[512,256]{1,0:T(8,128)(2,1)S(1)} %collective-permute-done.1.refs_1_.refs_2_, ...), custom_call_target="tpu_custom_call" | custom-call | tf_op jit(solution)/shard_map/pallas_call | solution.py:204
  54.8 4.7 %collective-permute-start.7 = (bf16[2,512,256]{2,1,0:T(8,128)(2,1)S(1)}, bf16[2,512,256]{2,1,0:T(8,128)(2,1)S(1)}, u32[]{:S(2)}, u32[]{:S(2)}) collective-permute-start(bf16[2,512,256]{2,1,0:T(8,128)(2,1)S(1)} %get-tuple-element.4.refs_8_), channel_id=1, source_target_pairs={{0,128},{128,0},{1,129},{129,1},{2,130},{130,2},{3,131},{131,3},{4... | collective-permute-start | bytes 1572872 | tf_op jit(solution)/shard_map/ppermute | solution.py:217
  59.6 0.7 broadcast_in_dim.19
  60.3 12.0 %all-to-all-start.2 = ((f32[8,16,512]{2,1,0:T(8,128)}), f32[8,16,512]{2,1,0:T(8,128)}, u32[]{:S(2)}, u32[]{:S(2)}) async-start(f32[8,16,512]{2,1,0:T(8,128)} %broadcast_in_dim.19), calls=%async_computation.2 | async-start | bytes 524288 | tf_op jit(solution)/shard_map/all_to_all | solution.py:191
  72.2 2.0 %collective-permute-start.10 = (bf16[512,256]{1,0:T(8,128)(2,1)}, bf16[512,256]{1,0:T(8,128)(2,1)}, u32[]{:S(2)}, u32[]{:S(2)}) collective-permute-start(bf16[512,256]{1,0:T(8,128)(2,1)} %get-tuple-element.5.refs_12_), channel_id=1, source_target_pairs={{0,128},{128,0},{1,129},{129,1},{2,130},{130,2},{3,131},{131,3},{4... | collective-permute-start | bytes 786440 | tf_op jit(solution)/shard_map/ppermute | solution.py:220
  74.3 8.5 %collective-permute-start.6 = (bf16[2,512,256]{2,1,0:T(8,128)(2,1)S(1)}, bf16[2,512,256]{2,1,0:T(8,128)(2,1)S(1)}, u32[]{:S(2)}, u32[]{:S(2)}) collective-permute-start(bf16[2,512,256]{2,1,0:T(8,128)(2,1)S(1)} %get-tuple-element.4.refs_8_), channel_id=1, source_target_pairs={{0,64},{64,0},{1,65},{65,1},{2,66},{66,2},{3,67},{67,3},{4,68},{68... | collective-permute-start | bytes 1572872 | tf_op jit(solution)/shard_map/ppermute | solution.py:218
  82.8 1.9 %collective-permute-start.9 = (bf16[512,256]{1,0:T(8,128)(2,1)}, bf16[512,256]{1,0:T(8,128)(2,1)}, u32[]{:S(2)}, u32[]{:S(2)}) collective-permute-start(bf16[512,256]{1,0:T(8,128)(2,1)} %get-tuple-element.5.refs_12_), channel_id=1, source_target_pairs={{0,64},{64,0},{1,65},{65,1},{2,66},{66,2},{3,67},{67,3},{4,68},{68... | collective-permute-start | bytes 786440 | tf_op jit(solution)/shard_map/ppermute | solution.py:221
  84.7 6.5 %collective-permute-start.11 = (bf16[512,256]{1,0:T(8,128)(2,1)}, bf16[512,256]{1,0:T(8,128)(2,1)}, u32[]{:S(2)}, u32[]{:S(2)}) collective-permute-start(bf16[512,256]{1,0:T(8,128)(2,1)} %collective-permute-done.10.refs_14_), channel_id=1, source_target_pairs={{0,64},{64,0},{1,65},{65,1},{2,66},{66,2},{3,67},{67,3},{4,68},{68... | collective-permute-start | bytes 786440 | tf_op jit(solution)/shard_map/ppermute | solution.py:222
  91.3 1.0 %fusion.10 = (bf16[128,512]{1,0:T(8,128)(2,1)S(1)}, bf16[128,512]{1,0:T(8,128)(2,1)S(1)}) fusion(f32[8,16,512]{2,1,0:T(8,128)} %all-to-all-done.2), kind=kLoop, calls=%fused_computation.15 | loop fusion | flops 262144 | bytes 524288 | tf_op jit(solution)/shard_map/convert_element_type | solution.py:193
  92.5 0.8 fusion.3
  93.4 4.0 %shard_map.42 = bf16[3,256,1024]{2,1,0:T(8,128)(2,1)} custom-call(s32[4096]{0:T(1024)S(1)} %copy-done, bf16[512,256]{1,0:T(8,128)(2,1)S(1)} %collective-permute-done.refs_0_.refs_1_, bf16[512,256]{1,0:T(8,128)(2,1)S(1)} %collective-permute-done.1.refs_1_.refs_2_, bf16[512,256]{1,0:T(8,128)(2,1)S(1)} %collective-permute-done.2.refs_2_.refs_3_, ...), custom_call_target="tpu_custom_call" | custom-call | tf_op jit(solution)/shard_map/pallas_call | solution.py:223
  (26 shorter events, 0.6 us)
Async XLA Ops:
  9.7 43.4 %copy-start = (s32[4096]{0:T(1024)S(1)}, s32[4096]{0:T(1024)}, u32[]{:S(2)}) copy-start(s32[4096]{0:T(1024)} %constant.18.clone.table_ref.refs_0_) | copy-start | bytes 49156
  11.7 28.7 %all-to-all-start = ((f32[8,16,512]{2,1,0:T(8,128)}), f32[8,16,512]{2,1,0:T(8,128)S(1)}, u32[]{:S(2)}, u32[]{:S(2)}) async-start(f32[8,16,512]{2,1,0:T(8,128)} %bitcast), calls=%async_computation | async-start | bytes 524288 | tf_op jit(solution)/shard_map/all_to_all | solution.py:189
  18.2 21.5 %collective-permute-start = (bf16[512,256]{1,0:T(8,128)(2,1)S(1)}, bf16[512,256]{1,0:T(8,128)(2,1)S(1)}, u32[]{:S(2)}, u32[]{:S(2)}) collective-permute-start(bf16[512,256]{1,0:T(8,128)(2,1)S(1)} %get-tuple-element.8.refs_6_.refs_7_), channel_id=1, source_target_pairs={{0,4},{1,75},{2,133},{3,206},{4,30},{5,65},{6,155},{7,218},{8,36},... | collective-permute-start | bytes 786440 | tf_op jit(solution)/shard_map/ppermute | solution.py:180
  23.1 23.7 %collective-permute-start.1 = (bf16[512,256]{1,0:T(8,128)(2,1)S(1)}, bf16[512,256]{1,0:T(8,128)(2,1)S(1)}, u32[]{:S(2)}, u32[]{:S(2)}) collective-permute-start(bf16[512,256]{1,0:T(8,128)(2,1)S(1)} %get-tuple-element.8.refs_6_.refs_7_), channel_id=1, source_target_pairs={{0,8},{1,67},{2,141},{3,194},{4,26},{5,83},{6,151},{7,214},{8,32},... | collective-permute-start | bytes 786440 | tf_op jit(solution)/shard_map/ppermute | solution.py:180
  31.9 17.9 %collective-permute-start.2 = (bf16[512,256]{1,0:T(8,128)(2,1)S(1)}, bf16[512,256]{1,0:T(8,128)(2,1)S(1)}, u32[]{:S(2)}, u32[]{:S(2)}) collective-permute-start(bf16[512,256]{1,0:T(8,128)(2,1)S(1)} %get-tuple-element.8.refs_6_.refs_7_), channel_id=1, source_target_pairs={{0,12},{1,79},{2,137},{3,198},{4,18},{5,91},{6,129},{7,222},{8,40}... | collective-permute-start | bytes 786440 | tf_op jit(solution)/shard_map/ppermute | solution.py:180
  33.8 16.0 %collective-permute-start.3 = (bf16[512,256]{1,0:T(8,128)(2,1)S(1)}, bf16[512,256]{1,0:T(8,128)(2,1)S(1)}, u32[]{:S(2)}, u32[]{:S(2)}) collective-permute-start(bf16[512,256]{1,0:T(8,128)(2,1)S(1)} %get-tuple-element.8.refs_6_.refs_7_), channel_id=1, source_target_pairs={{2,129},{3,202},{4,22},{5,87},{6,147},{7,210},{8,44},{9,105},{10,1... | collective-permute-start | bytes 786440 | tf_op jit(solution)/shard_map/ppermute | solution.py:180
  38.4 14.7 %collective-permute-start.4 = (bf16[512,256]{1,0:T(8,128)(2,1)S(1)}, bf16[512,256]{1,0:T(8,128)(2,1)S(1)}, u32[]{:S(2)}, u32[]{:S(2)}) collective-permute-start(bf16[512,256]{1,0:T(8,128)(2,1)S(1)} %get-tuple-element.8.refs_6_.refs_7_), channel_id=1, source_target_pairs={{1,71},{26,135},{46,129},{48,2},{49,65},{51,194},{52,4},{53,67},{5... | collective-permute-start | bytes 786440 | tf_op jit(solution)/shard_map/ppermute | solution.py:180
  39.8 13.4 %collective-permute-start.5 = (bf16[512,256]{1,0:T(8,128)(2,1)S(1)}, bf16[512,256]{1,0:T(8,128)(2,1)S(1)}, u32[]{:S(2)}, u32[]{:S(2)}) collective-permute-start(bf16[512,256]{1,0:T(8,128)(2,1)S(1)} %get-tuple-element.8.refs_6_.refs_7_), channel_id=1, source_target_pairs={{50,129},{176,1},{179,193}} | collective-permute-start | bytes 786440 | tf_op jit(solution)/shard_map/ppermute | solution.py:180
  41.2 18.3 %all-to-all-start.1 = ((f32[8,16,512]{2,1,0:T(8,128)}), f32[8,16,512]{2,1,0:T(8,128)S(1)}, u32[]{:S(2)}, u32[]{:S(2)}) async-start(f32[8,16,512]{2,1,0:T(8,128)} %broadcast_in_dim.18), calls=%async_computation.1 | async-start | bytes 524288 | tf_op jit(solution)/shard_map/all_to_all | solution.py:190
  46.8 45.7 %copy-start.1 = (bf16[128,256]{1,0:T(8,128)(2,1)S(1)}, bf16[128,256]{1,0:T(8,128)(2,1)}, u32[]{:S(2)}) copy-start(bf16[128,256]{1,0:T(8,128)(2,1)} %param.2) | copy-start | bytes 196612
  54.8 36.4 %collective-permute-start.7 = (bf16[2,512,256]{2,1,0:T(8,128)(2,1)S(1)}, bf16[2,512,256]{2,1,0:T(8,128)(2,1)S(1)}, u32[]{:S(2)}, u32[]{:S(2)}) collective-permute-start(bf16[2,512,256]{2,1,0:T(8,128)(2,1)S(1)} %get-tuple-element.4.refs_8_), channel_id=1, source_target_pairs={{0,128},{128,0},{1,129},{129,1},{2,130},{130,2},{3,131},{131,3},{4... | collective-permute-start | bytes 1572872 | tf_op jit(solution)/shard_map/ppermute | solution.py:217
  60.3 31.1 %all-to-all-start.2 = ((f32[8,16,512]{2,1,0:T(8,128)}), f32[8,16,512]{2,1,0:T(8,128)}, u32[]{:S(2)}, u32[]{:S(2)}) async-start(f32[8,16,512]{2,1,0:T(8,128)} %broadcast_in_dim.19), calls=%async_computation.2 | async-start | bytes 524288 | tf_op jit(solution)/shard_map/all_to_all | solution.py:191
  72.2 12.5 %collective-permute-start.10 = (bf16[512,256]{1,0:T(8,128)(2,1)}, bf16[512,256]{1,0:T(8,128)(2,1)}, u32[]{:S(2)}, u32[]{:S(2)}) collective-permute-start(bf16[512,256]{1,0:T(8,128)(2,1)} %get-tuple-element.5.refs_12_), channel_id=1, source_target_pairs={{0,128},{128,0},{1,129},{129,1},{2,130},{130,2},{3,131},{131,3},{4... | collective-permute-start | bytes 786440 | tf_op jit(solution)/shard_map/ppermute | solution.py:220
  74.3 19.0 %collective-permute-start.6 = (bf16[2,512,256]{2,1,0:T(8,128)(2,1)S(1)}, bf16[2,512,256]{2,1,0:T(8,128)(2,1)S(1)}, u32[]{:S(2)}, u32[]{:S(2)}) collective-permute-start(bf16[2,512,256]{2,1,0:T(8,128)(2,1)S(1)} %get-tuple-element.4.refs_8_), channel_id=1, source_target_pairs={{0,64},{64,0},{1,65},{65,1},{2,66},{66,2},{3,67},{67,3},{4,68},{68... | collective-permute-start | bytes 1572872 | tf_op jit(solution)/shard_map/ppermute | solution.py:218
  82.8 10.6 %collective-permute-start.9 = (bf16[512,256]{1,0:T(8,128)(2,1)}, bf16[512,256]{1,0:T(8,128)(2,1)}, u32[]{:S(2)}, u32[]{:S(2)}) collective-permute-start(bf16[512,256]{1,0:T(8,128)(2,1)} %get-tuple-element.5.refs_12_), channel_id=1, source_target_pairs={{0,64},{64,0},{1,65},{65,1},{2,66},{66,2},{3,67},{67,3},{4,68},{68... | collective-permute-start | bytes 786440 | tf_op jit(solution)/shard_map/ppermute | solution.py:221
  84.7 8.7 %collective-permute-start.11 = (bf16[512,256]{1,0:T(8,128)(2,1)}, bf16[512,256]{1,0:T(8,128)(2,1)}, u32[]{:S(2)}, u32[]{:S(2)}) collective-permute-start(bf16[512,256]{1,0:T(8,128)(2,1)} %collective-permute-done.10.refs_14_), channel_id=1, source_target_pairs={{0,64},{64,0},{1,65},{65,1},{2,66},{66,2},{3,67},{67,3},{4,68},{68... | collective-permute-start | bytes 786440 | tf_op jit(solution)/shard_map/ppermute | solution.py:222
  91.2 2.2 %collective-permute-start.8 = (bf16[2,512,256]{2,1,0:T(8,128)(2,1)S(1)}, bf16[2,512,256]{2,1,0:T(8,128)(2,1)}, u32[]{:S(2)}, u32[]{:S(2)}) collective-permute-start(bf16[2,512,256]{2,1,0:T(8,128)(2,1)S(1)} %collective-permute-done.7.refs_10_), channel_id=1, source_target_pairs={{0,64},{64,0},{1,65},{65,1},{2,66},{66,2},{3,67},{67,3},{4,68},{68... | collective-permute-start | bytes 1572872 | tf_op jit(solution)/shard_map/ppermute | solution.py:219
where the time goes:
time: 98.1 us; the launch traced here: 97.4 us
  starting transfers between devices  70 us (71%)
  blocking collectives  9.07 us (9%)
  waiting for transfers between devices  6.28 us (6%)
  Pallas kernels  5.71 us (6%)
  matrix products  2.79 us (3%)
  local copies, waits for them, and re-layouts  1.47 us (1%)
  other arithmetic  1.28 us (1%)
    ppermute x6, starting transfers between devices, shards(): arrived = [lax.ppermute(centered, EVERY, pairs) for pairs in rounds]  22.2 us
    all_to_all x1, starting transfers between devices, shards(): lax.all_to_all(jnp.broadcast_to(part, (8, *part.shape)), 'z', 0, 0)  12 us
    all_gather x1, blocking collectives, shards(): lax.all_gather(embedding, BATCH, axis=0, tiled=True).astype(jnp.float32)  9.07 us
    ppermute x1, starting transfers between devices, shards(): right_c = lax.ppermute(right, 'co', swap)  8.45 us
    ppermute x1, starting transfers between devices, shards(): last_yc = lax.ppermute(last_y, ('co', 'z'), swap_first)  6.49 us
    all_to_all x1, starting transfers between devices, shards(): part = lax.all_to_all(gram.reshape(8, -1, row_count), 'z', 0, 0).sum(0)  6.49 us
    ppermute x6, waiting for transfers between devices, shards(): arrived = [lax.ppermute(centered, EVERY, pairs) for pairs in rounds]  6.26 us
    all_to_all x1, starting transfers between devices, shards(): lax.all_to_all(jnp.broadcast_to(part, (8, *part.shape)), ('x', 'yh'), 0, 0)  5.64 us
  transfers between devices with their start and end apart: 15, of which 2 were waited for; matrix products, arithmetic and copies ran while one was open for 4% of the time, Pallas kernels for 2%

commit v1 on v0

--- a/solution.py
+++ b/solution.py
@@ -122,9 +122,9 @@
 
 
 def pick_kernel(table_ref, *refs):
-    sources, (right_ref, last_ref, sems) = refs[:-3], refs[-3:]
+    sources, (right_ref, sems) = refs[:-2], refs[-2:]
     entry = my_entries(table_ref)
-    targets = [right_ref.at[0], right_ref.at[1], last_ref]
+    targets = [right_ref.at[k] for k in range(SLOTS)]
     for k in range(SLOTS):
         fetch(entry[2 * k + 1], sources, targets[k], sems.at[k])
     for k in range(SLOTS):
@@ -132,7 +132,7 @@
 
 
 def tile_kernel(scale, table_ref, *refs):
-    sources, rights, lasts = refs[:-11], refs[-11:-7], refs[-7:-3]
+    sources, rights, lasts = refs[:-9], refs[-9:-5], refs[-5:-3]
     out_ref, left_ref, sems = refs[-3:]
     yl, co = lax.axis_index("yl"), lax.axis_index("co")
     entry = my_entries(table_ref)
@@ -158,7 +158,7 @@
 
     @pl.when(entry[4] >= 0)
     def _():
-        fill(2, lasts)
+        fill(2, [rights[0].at[2], rights[1].at[2], *lasts])
 
     @pl.when(entry[4] < 0)
     def _():
@@ -186,9 +186,9 @@
     gram = lax.dot_general(
         my_exact.astype(jnp.bfloat16), centered, (((1,), (1,)), ((), ())), preferred_element_type=jnp.float32
     )
-    part = lax.all_to_all(gram.reshape(8, -1, row_count), "z", 0, 0).sum(0)
-    part = lax.all_to_all(jnp.broadcast_to(part, (8, *part.shape)), ("x", "yh"), 0, 0).sum(0)
-    gram = lax.all_to_all(jnp.broadcast_to(part, (8, *part.shape)), "z", 0, 0).reshape(local_rows, row_count)
+    part = lax.all_to_all(gram.reshape(8, -1, row_count), ("x", "yh"), 0, 0).sum(0)
+    part = lax.all_to_all(jnp.broadcast_to(part, (8, *part.shape)), "z", 0, 0).sum(0)
+    gram = lax.all_to_all(jnp.broadcast_to(part, (8, *part.shape)), ("x", "yh"), 0, 0).reshape(local_rows, row_count)
     gram_hi = lax.reduce_precision(gram, 8, 7)
     gram_lo = (gram - gram_hi).astype(jnp.bfloat16)
     whole = jnp.dot(gram_hi.astype(jnp.bfloat16), centered, preferred_element_type=jnp.float32)
@@ -201,36 +201,32 @@
     anywhere = pl.BlockSpec(memory_space=pl.ANY)
     vmem = pl.BlockSpec(memory_space=pltpu.VMEM)
     smem = pl.BlockSpec(memory_space=pltpu.SMEM)
-    right, last = pl.pallas_call(
+    swap = [(0, 1), (1, 0)]
+    swap_first = [(0, 8), (8, 0)]
+    right = pl.pallas_call(
         pick_kernel,
-        out_shape=(
-            jax.ShapeDtypeStruct((2, row_count, PIECE), jnp.bfloat16),
-            jax.ShapeDtypeStruct((row_count, PIECE), jnp.bfloat16),
-        ),
+        out_shape=jax.ShapeDtypeStruct((3, row_count, PIECE), jnp.bfloat16),
         in_specs=[smem] + [anywhere] * len(sources),
-        out_specs=(vmem, vmem),
+        out_specs=vmem,
         scratch_shapes=[pltpu.SemaphoreType.DMA((SLOTS,))],
         compiler_params=pltpu.CompilerParams(vmem_limit_bytes=16 * 2**20),
     )(table, *sources)
-    swap = [(0, 1), (1, 0)]
-    swap_first = [(0, 8), (8, 0)]
-    right_y = lax.ppermute(right, "yl", swap)
+    right_y = lax.ppermute(right[:2], "yl", swap)
+    last_y = lax.ppermute(right[2], ("yl", "z"), swap_first)
     right_c = lax.ppermute(right, "co", swap)
     right_yc = lax.ppermute(right_y, "co", swap)
-    last_y = lax.ppermute(last, ("yl", "z"), swap_first)
-    last_c = lax.ppermute(last, ("co", "z"), swap_first)
     last_yc = lax.ppermute(last_y, ("co", "z"), swap_first)
     tiles = pl.pallas_call(
         lambda *refs: tile_kernel(row_count - 1, *refs),
         out_shape=jax.ShapeDtypeStruct((SLOTS, PIECE, BLK), jnp.bfloat16),
-        in_specs=[smem] + [anywhere] * len(sources) + [vmem] * 8,
+        in_specs=[smem] + [anywhere] * len(sources) + [vmem] * 6,
         out_specs=vmem,
         scratch_shapes=[
             pltpu.VMEM((SLOTS, row_count, PIECE), jnp.bfloat16),
             pltpu.SemaphoreType.DMA((SLOTS,)),
         ],
         compiler_params=pltpu.CompilerParams(vmem_limit_bytes=32 * 2**20),
-    )(table, *sources, right, right_c, right_y, right_yc, last, last_c, last_y, last_yc)
+    )(table, *sources, right, right_c, right_y, right_yc, last_y, last_yc)
     return grad, tiles
 
 

time: 98.1 us -> 92.5 us (0.943)
  the two profiles are of different devices: /device:TPU:1 before, /device:TPU:25 now
where the time goes in v1:
time: 92.5 us; the launch traced here: 91.7 us
  starting transfers between devices  56.6 us (61%)
  waiting for transfers between devices  15.8 us (17%)
  blocking collectives  6.51 us (7%)
  Pallas kernels  4.98 us (5%)
  local copies, waits for them, and re-layouts  3.01 us (3%)
  matrix products  2.78 us (3%)
  other arithmetic  1.28 us (1%)
    ppermute x6, starting transfers between devices, shards(): arrived = [lax.ppermute(centered, EVERY, pairs) for pairs in rounds]  21.7 us
    all_to_all x1, starting transfers between devices, shards(): lax.all_to_all(jnp.broadcast_to(part, (8, *part.shape)), 'z', 0, 0).sum(0)  9.97 us
    ppermute x6, waiting for transfers between devices, shards(): arrived = [lax.ppermute(centered, EVERY, pairs) for pairs in rounds]  8.66 us
    all_to_all x1, starting transfers between devices, shards(): lax.all_to_all(gram.reshape(8, -1, row_count), ('x', 'yh'), 0, 0).sum(0)  8.6 us
    ppermute x1, waiting for transfers between devices, shards(): last_y = lax.ppermute(right[2], ('yl', 'z'), swap_first)  6.91 us
    all_gather x1, blocking collectives, shards(): lax.all_gather(embedding, BATCH, axis=0, tiled=True).astype(jnp.float32)  6.51 us
    ppermute x1, starting transfers between devices, shards(): last_yc = lax.ppermute(last_y, ('co', 'z'), swap_first)  4.66 us
    all_to_all x1, starting transfers between devices, shards(): lax.all_to_all(jnp.broadcast_to(part, (8, *part.shape)), ('x', 'yh'), 0, 0)  4.24 us
  transfers between devices with their start and end apart: 14, of which 3 were waited for; matrix products, arithmetic and copies ran while one was open for 7% of the time, Pallas kernels for 1%

profile of v1, /device:TPU:25, one launch (start us, length us, event | category | flops | bytes accessed | tf_op | source)
XLA Modules:
  0.0 91.7 jit_solution(8202746922957406746)
XLA Ops:
  0.6 6.5 %all_gather.3 = bf16[512,256]{1,0:T(8,128)(2,1)S(1)} all-gather(bf16[128,256]{1,0:T(8,128)(2,1)} %param.2), channel_id=1, replica_groups=mesh['yl'=2,'co'=2,'z'=8,'x'=4,'yh'=2] {'yl','co'}, dimensions={0}, use_global_device_ids=true | all-gather | bytes 327680 | tf_op jit(solution)/shard_map/all_gather | solution.py:174
  7.4 4.4 %collective-permute-start = (bf16[512,256]{1,0:T(8,128)(2,1)S(1)}, bf16[512,256]{1,0:T(8,128)(2,1)S(1)}, u32[]{:S(2)}, u32[]{:S(2)}) collective-permute-start(bf16[512,256]{1,0:T(8,128)(2,1)S(1)} %get-tuple-element.4.refs_6_.refs_7_), channel_id=1, source_target_pairs={{0,4},{1,75},{2,133},{3,206},{4,30},{5,65},{6,155},{7,218},{8,36},... | collective-permute-start | bytes 786440 | tf_op jit(solution)/shard_map/ppermute | solution.py:180
  11.7 1.8 %fusion.13 = f32[128,512]{1,0:T(8,128)} fusion(bf16[512,256]{1,0:T(8,128)(2,1)S(1)} %get-tuple-element.4.refs_6_.refs_7_, bf16[128,256]{1,0:T(8,128)(2,1)} %param.2, f32[256]{0:T(256)S(1)} %broadcast_multiply_fusion), kind=kOutput, calls=%fused_computation.20 | convolution fusion | flops 33685504 | bytes 590848 | tf_op jit(solution)/shard_map/dot_general | solution.py:186
  13.5 8.6 %all-to-all-start = ((f32[8,16,512]{2,1,0:T(8,128)}), f32[8,16,512]{2,1,0:T(8,128)S(1)}, u32[]{:S(2)}, u32[]{:S(2)}) async-start(f32[8,16,512]{2,1,0:T(8,128)} %bitcast), calls=%async_computation | async-start | bytes 524288 | tf_op jit(solution)/shard_map/all_to_all | solution.py:189
  22.1 4.4 %collective-permute-start.1 = (bf16[512,256]{1,0:T(8,128)(2,1)S(1)}, bf16[512,256]{1,0:T(8,128)(2,1)S(1)}, u32[]{:S(2)}, u32[]{:S(2)}) collective-permute-start(bf16[512,256]{1,0:T(8,128)(2,1)S(1)} %get-tuple-element.4.refs_6_.refs_7_), channel_id=1, source_target_pairs={{0,8},{1,67},{2,141},{3,194},{4,26},{5,83},{6,151},{7,214},{8,32},... | collective-permute-start | bytes 786440 | tf_op jit(solution)/shard_map/ppermute | solution.py:180
  26.5 5.1 %collective-permute-start.2 = (bf16[512,256]{1,0:T(8,128)(2,1)S(1)}, bf16[512,256]{1,0:T(8,128)(2,1)S(1)}, u32[]{:S(2)}, u32[]{:S(2)}) collective-permute-start(bf16[512,256]{1,0:T(8,128)(2,1)S(1)} %get-tuple-element.4.refs_6_.refs_7_), channel_id=1, source_target_pairs={{0,12},{1,79},{2,137},{3,198},{4,18},{5,91},{6,129},{7,222},{8,40}... | collective-permute-start | bytes 786440 | tf_op jit(solution)/shard_map/ppermute | solution.py:180
  31.6 5.3 %collective-permute-start.3 = (bf16[512,256]{1,0:T(8,128)(2,1)S(1)}, bf16[512,256]{1,0:T(8,128)(2,1)S(1)}, u32[]{:S(2)}, u32[]{:S(2)}) collective-permute-start(bf16[512,256]{1,0:T(8,128)(2,1)S(1)} %get-tuple-element.4.refs_6_.refs_7_), channel_id=1, source_target_pairs={{2,129},{3,202},{4,22},{5,87},{6,147},{7,210},{8,44},{9,105},{10,1... | collective-permute-start | bytes 786440 | tf_op jit(solution)/shard_map/ppermute | solution.py:180
  36.9 1.3 %collective-permute-start.4 = (bf16[512,256]{1,0:T(8,128)(2,1)S(1)}, bf16[512,256]{1,0:T(8,128)(2,1)S(1)}, u32[]{:S(2)}, u32[]{:S(2)}) collective-permute-start(bf16[512,256]{1,0:T(8,128)(2,1)S(1)} %get-tuple-element.4.refs_6_.refs_7_), channel_id=1, source_target_pairs={{1,71},{26,135},{46,129},{48,2},{49,65},{51,194},{52,4},{53,67},{5... | collective-permute-start | bytes 786440 | tf_op jit(solution)/shard_map/ppermute | solution.py:180
  38.2 1.3 %collective-permute-start.5 = (bf16[512,256]{1,0:T(8,128)(2,1)S(1)}, bf16[512,256]{1,0:T(8,128)(2,1)S(1)}, u32[]{:S(2)}, u32[]{:S(2)}) collective-permute-start(bf16[512,256]{1,0:T(8,128)(2,1)S(1)} %get-tuple-element.4.refs_6_.refs_7_), channel_id=1, source_target_pairs={{50,129},{176,1},{179,193}} | collective-permute-start | bytes 786440 | tf_op jit(solution)/shard_map/ppermute | solution.py:180
  39.5 0.7 broadcast_in_dim.18
  40.3 10.0 %all-to-all-start.1 = ((f32[8,16,512]{2,1,0:T(8,128)}), f32[8,16,512]{2,1,0:T(8,128)S(1)}, u32[]{:S(2)}, u32[]{:S(2)}) async-start(f32[8,16,512]{2,1,0:T(8,128)} %broadcast_in_dim.18), calls=%async_computation.1 | async-start | bytes 524288 | tf_op jit(solution)/shard_map/all_to_all | solution.py:190
  50.3 8.7 %collective-permute-done.4.refs_4_.refs_5_ = bf16[512,256]{1,0:T(8,128)(2,1)S(1)} collective-permute-done((bf16[512,256]{1,0:T(8,128)(2,1)S(1)}, bf16[512,256]{1,0:T(8,128)(2,1)S(1)}, u32[]{:S(2)}, u32[]{:S(2)}) %collective-permute-start.4) | collective-permute-done | bytes 262176 | tf_op jit(solution)/shard_map/ppermute | solution.py:180
  58.9 1.0 %shard_map.41.refs_8_ = bf16[3,512,256]{2,1,0:T(8,128)(2,1)S(1)} custom-call(s32[4096]{0:T(1024)S(1)} %copy-done, bf16[512,256]{1,0:T(8,128)(2,1)S(1)} %collective-permute-done.refs_0_.refs_1_, bf16[512,256]{1,0:T(8,128)(2,1)S(1)} %collective-permute-done.1.refs_1_.refs_2_, bf16[512,256]{1,0:T(8,128)(2,1)S(1)} %collective-permute-done.2.refs_2_.refs_3_, ...), custom_call_target="tpu_custom_call" | custom-call | tf_op jit(solution)/shard_map/pallas_call | solution.py:206
  59.9 0.8 slice.8
  60.8 0.7 slice_bitcast_fusion
  61.5 3.4 %collective-permute-start.9 = (bf16[512,256]{1,0:T(8,128)(2,1)}, bf16[512,256]{1,0:T(8,128)(2,1)}, u32[]{:S(2)}, u32[]{:S(2)}) collective-permute-start(bf16[512,256]{1,0:T(8,128)(2,1)} %slice_bitcast_fusion), channel_id=1, source_target_pairs={{0,128},{128,0},{1,129},{129,1},{2,130},{130,2},{3,131},{131,3},{4... | collective-permute-start | bytes 786440 | tf_op jit(solution)/shard_map/ppermute | solution.py:215
  64.9 0.7 broadcast_in_dim.19
  65.6 4.2 %all-to-all-start.2 = ((f32[8,16,512]{2,1,0:T(8,128)}), f32[8,16,512]{2,1,0:T(8,128)}, u32[]{:S(2)}, u32[]{:S(2)}) async-start(f32[8,16,512]{2,1,0:T(8,128)} %broadcast_in_dim.19), calls=%async_computation.2 | async-start | bytes 524288 | tf_op jit(solution)/shard_map/all_to_all | solution.py:191
  69.9 3.9 %collective-permute-start.6 = (bf16[3,512,256]{2,1,0:T(8,128)(2,1)S(1)}, bf16[3,512,256]{2,1,0:T(8,128)(2,1)S(1)}, u32[]{:S(2)}, u32[]{:S(2)}) collective-permute-start(bf16[3,512,256]{2,1,0:T(8,128)(2,1)S(1)} %shard_map.41.refs_8_), channel_id=1, source_target_pairs={{0,64},{64,0},{1,65},{65,1},{2,66},{66,2},{3,67},{67,3},{4,68},{68... | collective-permute-start | bytes 2359304 | tf_op jit(solution)/shard_map/ppermute | solution.py:216
  73.8 6.9 %collective-permute-done.9.refs_12_ = bf16[512,256]{1,0:T(8,128)(2,1)} collective-permute-done((bf16[512,256]{1,0:T(8,128)(2,1)}, bf16[512,256]{1,0:T(8,128)(2,1)}, u32[]{:S(2)}, u32[]{:S(2)}) %collective-permute-start.9) | collective-permute-done | bytes 262176 | tf_op jit(solution)/shard_map/ppermute | solution.py:215
  80.7 4.7 %collective-permute-start.10 = (bf16[512,256]{1,0:T(8,128)(2,1)}, bf16[512,256]{1,0:T(8,128)(2,1)}, u32[]{:S(2)}, u32[]{:S(2)}) collective-permute-start(bf16[512,256]{1,0:T(8,128)(2,1)} %collective-permute-done.9.refs_12_), channel_id=1, source_target_pairs={{0,64},{64,0},{1,65},{65,1},{2,66},{66,2},{3,67},{67,3},{4,68},{68... | collective-permute-start | bytes 786440 | tf_op jit(solution)/shard_map/ppermute | solution.py:218
  85.5 1.0 %fusion.10 = (bf16[128,512]{1,0:T(8,128)(2,1)S(1)}, bf16[128,512]{1,0:T(8,128)(2,1)S(1)}) fusion(f32[8,16,512]{2,1,0:T(8,128)} %all-to-all-done.2), kind=kLoop, calls=%fused_computation.15 | loop fusion | flops 262144 | bytes 524288 | tf_op jit(solution)/shard_map/convert_element_type | solution.py:193
  86.7 0.8 fusion.3
  87.8 4.0 %shard_map.42 = bf16[3,256,1024]{2,1,0:T(8,128)(2,1)} custom-call(s32[4096]{0:T(1024)S(1)} %copy-done, bf16[512,256]{1,0:T(8,128)(2,1)S(1)} %collective-permute-done.refs_0_.refs_1_, bf16[512,256]{1,0:T(8,128)(2,1)S(1)} %collective-permute-done.1.refs_1_.refs_2_, bf16[512,256]{1,0:T(8,128)(2,1)S(1)} %collective-permute-done.2.refs_2_.refs_3_, ...), custom_call_target="tpu_custom_call" | custom-call | tf_op jit(solution)/shard_map/pallas_call | solution.py:219
  (26 shorter events, 0.8 us)
Async XLA Ops:
  7.1 51.8 %copy-start = (s32[4096]{0:T(1024)S(1)}, s32[4096]{0:T(1024)}, u32[]{:S(2)}) copy-start(s32[4096]{0:T(1024)} %constant.18.clone.table_ref.refs_0_) | copy-start | bytes 49156
  7.4 30.8 %collective-permute-start = (bf16[512,256]{1,0:T(8,128)(2,1)S(1)}, bf16[512,256]{1,0:T(8,128)(2,1)S(1)}, u32[]{:S(2)}, u32[]{:S(2)}) collective-permute-start(bf16[512,256]{1,0:T(8,128)(2,1)S(1)} %get-tuple-element.4.refs_6_.refs_7_), channel_id=1, source_target_pairs={{0,4},{1,75},{2,133},{3,206},{4,30},{5,65},{6,155},{7,218},{8,36},... | collective-permute-start | bytes 786440 | tf_op jit(solution)/shard_map/ppermute | solution.py:180
  13.5 26.0 %all-to-all-start = ((f32[8,16,512]{2,1,0:T(8,128)}), f32[8,16,512]{2,1,0:T(8,128)S(1)}, u32[]{:S(2)}, u32[]{:S(2)}) async-start(f32[8,16,512]{2,1,0:T(8,128)} %bitcast), calls=%async_computation | async-start | bytes 524288 | tf_op jit(solution)/shard_map/all_to_all | solution.py:189
  22.1 28.1 %collective-permute-start.1 = (bf16[512,256]{1,0:T(8,128)(2,1)S(1)}, bf16[512,256]{1,0:T(8,128)(2,1)S(1)}, u32[]{:S(2)}, u32[]{:S(2)}) collective-permute-start(bf16[512,256]{1,0:T(8,128)(2,1)S(1)} %get-tuple-element.4.refs_6_.refs_7_), channel_id=1, source_target_pairs={{0,8},{1,67},{2,141},{3,194},{4,26},{5,83},{6,151},{7,214},{8,32},... | collective-permute-start | bytes 786440 | tf_op jit(solution)/shard_map/ppermute | solution.py:180
  26.5 23.8 %collective-permute-start.2 = (bf16[512,256]{1,0:T(8,128)(2,1)S(1)}, bf16[512,256]{1,0:T(8,128)(2,1)S(1)}, u32[]{:S(2)}, u32[]{:S(2)}) collective-permute-start(bf16[512,256]{1,0:T(8,128)(2,1)S(1)} %get-tuple-element.4.refs_6_.refs_7_), channel_id=1, source_target_pairs={{0,12},{1,79},{2,137},{3,198},{4,18},{5,91},{6,129},{7,222},{8,40}... | collective-permute-start | bytes 786440 | tf_op jit(solution)/shard_map/ppermute | solution.py:180
  31.6 18.6 %collective-permute-start.3 = (bf16[512,256]{1,0:T(8,128)(2,1)S(1)}, bf16[512,256]{1,0:T(8,128)(2,1)S(1)}, u32[]{:S(2)}, u32[]{:S(2)}) collective-permute-start(bf16[512,256]{1,0:T(8,128)(2,1)S(1)} %get-tuple-element.4.refs_6_.refs_7_), channel_id=1, source_target_pairs={{2,129},{3,202},{4,22},{5,87},{6,147},{7,210},{8,44},{9,105},{10,1... | collective-permute-start | bytes 786440 | tf_op jit(solution)/shard_map/ppermute | solution.py:180
  36.9 22.0 %collective-permute-start.4 = (bf16[512,256]{1,0:T(8,128)(2,1)S(1)}, bf16[512,256]{1,0:T(8,128)(2,1)S(1)}, u32[]{:S(2)}, u32[]{:S(2)}) collective-permute-start(bf16[512,256]{1,0:T(8,128)(2,1)S(1)} %get-tuple-element.4.refs_6_.refs_7_), channel_id=1, source_target_pairs={{1,71},{26,135},{46,129},{48,2},{49,65},{51,194},{52,4},{53,67},{5... | collective-permute-start | bytes 786440 | tf_op jit(solution)/shard_map/ppermute | solution.py:180
  38.2 20.7 %collective-permute-start.5 = (bf16[512,256]{1,0:T(8,128)(2,1)S(1)}, bf16[512,256]{1,0:T(8,128)(2,1)S(1)}, u32[]{:S(2)}, u32[]{:S(2)}) collective-permute-start(bf16[512,256]{1,0:T(8,128)(2,1)S(1)} %get-tuple-element.4.refs_6_.refs_7_), channel_id=1, source_target_pairs={{50,129},{176,1},{179,193}} | collective-permute-start | bytes 786440 | tf_op jit(solution)/shard_map/ppermute | solution.py:180
  40.3 24.6 %all-to-all-start.1 = ((f32[8,16,512]{2,1,0:T(8,128)}), f32[8,16,512]{2,1,0:T(8,128)S(1)}, u32[]{:S(2)}, u32[]{:S(2)}) async-start(f32[8,16,512]{2,1,0:T(8,128)} %broadcast_in_dim.18), calls=%async_computation.1 | async-start | bytes 524288 | tf_op jit(solution)/shard_map/all_to_all | solution.py:190
  60.8 25.9 %copy-start.1 = (bf16[128,256]{1,0:T(8,128)(2,1)S(1)}, bf16[128,256]{1,0:T(8,128)(2,1)}, u32[]{:S(2)}) copy-start(bf16[128,256]{1,0:T(8,128)(2,1)} %param.2) | copy-start | bytes 196612
  60.8 24.6 %collective-permute-start.7 = (bf16[2,512,256]{2,1,0:T(8,128)(2,1)}, bf16[2,512,256]{2,1,0:T(8,128)(2,1)}, u32[]{:S(2)}, u32[]{:S(2)}) collective-permute-start(bf16[2,512,256]{2,1,0:T(8,128)(2,1)} %slice.8), channel_id=1, source_target_pairs={{0,128},{128,0},{1,129},{129,1},{2,130},{130,2},{3,131},{131,3},{4... | collective-permute-start | bytes 1572872 | tf_op jit(solution)/shard_map/ppermute | solution.py:214
  61.5 19.3 %collective-permute-start.9 = (bf16[512,256]{1,0:T(8,128)(2,1)}, bf16[512,256]{1,0:T(8,128)(2,1)}, u32[]{:S(2)}, u32[]{:S(2)}) collective-permute-start(bf16[512,256]{1,0:T(8,128)(2,1)} %slice_bitcast_fusion), channel_id=1, source_target_pairs={{0,128},{128,0},{1,129},{129,1},{2,130},{130,2},{3,131},{131,3},{4... | collective-permute-start | bytes 786440 | tf_op jit(solution)/shard_map/ppermute | solution.py:215
  65.6 19.9 %all-to-all-start.2 = ((f32[8,16,512]{2,1,0:T(8,128)}), f32[8,16,512]{2,1,0:T(8,128)}, u32[]{:S(2)}, u32[]{:S(2)}) async-start(f32[8,16,512]{2,1,0:T(8,128)} %broadcast_in_dim.19), calls=%async_computation.2 | async-start | bytes 524288 | tf_op jit(solution)/shard_map/all_to_all | solution.py:191
  69.9 17.7 %collective-permute-start.6 = (bf16[3,512,256]{2,1,0:T(8,128)(2,1)S(1)}, bf16[3,512,256]{2,1,0:T(8,128)(2,1)S(1)}, u32[]{:S(2)}, u32[]{:S(2)}) collective-permute-start(bf16[3,512,256]{2,1,0:T(8,128)(2,1)S(1)} %shard_map.41.refs_8_), channel_id=1, source_target_pairs={{0,64},{64,0},{1,65},{65,1},{2,66},{66,2},{3,67},{67,3},{4,68},{68... | collective-permute-start | bytes 2359304 | tf_op jit(solution)/shard_map/ppermute | solution.py:216
  80.7 6.8 %collective-permute-start.10 = (bf16[512,256]{1,0:T(8,128)(2,1)}, bf16[512,256]{1,0:T(8,128)(2,1)}, u32[]{:S(2)}, u32[]{:S(2)}) collective-permute-start(bf16[512,256]{1,0:T(8,128)(2,1)} %collective-permute-done.9.refs_12_), channel_id=1, source_target_pairs={{0,64},{64,0},{1,65},{65,1},{2,66},{66,2},{3,67},{67,3},{4,68},{68... | collective-permute-start | bytes 786440 | tf_op jit(solution)/shard_map/ppermute | solution.py:218
  85.4 2.3 %collective-permute-start.8 = (bf16[2,512,256]{2,1,0:T(8,128)(2,1)}, bf16[2,512,256]{2,1,0:T(8,128)(2,1)}, u32[]{:S(2)}, u32[]{:S(2)}) collective-permute-start(bf16[2,512,256]{2,1,0:T(8,128)(2,1)} %collective-permute-done.7.refs_10_), channel_id=1, source_target_pairs={{0,64},{64,0},{1,65},{65,1},{2,66},{66,2},{3,67},{67,3},{4,68},{68... | collective-permute-start | bytes 1572872 | tf_op jit(solution)/shard_map/ppermute | solution.py:217

commit v2 on v1

--- a/solution.py
+++ b/solution.py
@@ -122,36 +122,45 @@
 
 
 def pick_kernel(table_ref, *refs):
-    sources, (right_ref, sems) = refs[:-2], refs[-2:]
+    sources, (right_ref, pair_ref, last_ref, sems) = refs[:-4], refs[-4:]
     entry = my_entries(table_ref)
-    targets = [right_ref.at[k] for k in range(SLOTS)]
-    for k in range(SLOTS):
-        fetch(entry[2 * k + 1], sources, targets[k], sems.at[k])
-    for k in range(SLOTS):
-        fetched(entry[2 * k + 1], sources[0], targets[k], sems.at[k])
+    jobs = [(1, pair_ref.at[0]), (3, pair_ref.at[1]), (5, last_ref)]
+    jobs += [(2 * k + 1, right_ref.at[k]) for k in range(SLOTS)]
+    for i, (e, target) in enumerate(jobs):
+        fetch(entry[e], sources, target, sems.at[i])
+    for i, (e, target) in enumerate(jobs):
+        fetched(entry[e], sources[0], target, sems.at[i])
 
 
 def tile_kernel(scale, table_ref, *refs):
-    sources, rights, lasts = refs[:-9], refs[-9:-5], refs[-5:-3]
-    out_ref, left_ref, sems = refs[-3:]
+    sources, rights, lasts = refs[:-11], refs[-11:-7], refs[-7:-5]
+    out_ref, left_ref, tile_ref, sems, out_sems = refs[-5:]
     yl, co = lax.axis_index("yl"), lax.axis_index("co")
     entry = my_entries(table_ref)
     for k in range(SLOTS):
         fetch(entry[2 * k], sources, left_ref.at[k], sems.at[k])
-    for k in range(SLOTS):
+
+    def send(k):
+        return pltpu.make_async_copy(tile_ref.at[k], out_ref.at[k], out_sems.at[k])
+
+    @pl.when(entry[4] < 0)
+    def _():
+        tile_ref[2] = jnp.zeros(tile_ref.shape[1:], tile_ref.dtype)
+        send(2).start()
+
+    def fill(k, pieces):
         fetched(entry[2 * k], sources[0], left_ref.at[k], sems.at[k])
-
-    def fill(k, pieces):
         left = left_ref[k].T
         for n, piece in enumerate(pieces):
             q = (yl ^ (n // 2)) * 2 + (co ^ (n % 2))
             cols = pl.ds(pl.multiple_of(q * PIECE, PIECE), PIECE)
-            cov = jnp.dot(left, piece[...], preferred_element_type=jnp.float32) / scale
+            cov = jnp.dot(left, piece[...], preferred_element_type=jnp.float32) * (1.0 / scale)
             on_diagonal = lax.broadcasted_iota(jnp.int32, cov.shape, 0) == lax.broadcasted_iota(
                 jnp.int32, cov.shape, 1
             )
             dropped = on_diagonal & (entry[2 * SLOTS + k] == 1) & (n == 0)
-            out_ref[k, :, cols] = jnp.where(dropped, 0.0, cov).astype(out_ref.dtype)
+            tile_ref[k, :, cols] = jnp.where(dropped, 0.0, cov).astype(tile_ref.dtype)
+        send(k).start()
 
     for k in range(2):
         fill(k, [piece.at[k] for piece in rights])
@@ -160,9 +169,8 @@
     def _():
         fill(2, [rights[0].at[2], rights[1].at[2], *lasts])
 
-    @pl.when(entry[4] < 0)
-    def _():
-        out_ref[2] = jnp.zeros(out_ref.shape[1:], out_ref.dtype)
+    for k in range(SLOTS):
+        send(k).wait()
 
 
 def shards(embedding):
@@ -187,7 +195,8 @@
         my_exact.astype(jnp.bfloat16), centered, (((1,), (1,)), ((), ())), preferred_element_type=jnp.float32
     )
     part = lax.all_to_all(gram.reshape(8, -1, row_count), ("x", "yh"), 0, 0).sum(0)
-    part = lax.all_to_all(jnp.broadcast_to(part, (8, *part.shape)), "z", 0, 0).sum(0)
+    part = part.astype(jnp.bfloat16)
+    part = lax.all_to_all(jnp.broadcast_to(part, (8, *part.shape)), "z", 0, 0).astype(jnp.float32).sum(0)
     gram = lax.all_to_all(jnp.broadcast_to(part, (8, *part.shape)), ("x", "yh"), 0, 0).reshape(local_rows, row_count)
     gram_hi = lax.reduce_precision(gram, 8, 7)
     gram_lo = (gram - gram_hi).astype(jnp.bfloat16)
@@ -203,16 +212,20 @@
     smem = pl.BlockSpec(memory_space=pltpu.SMEM)
     swap = [(0, 1), (1, 0)]
     swap_first = [(0, 8), (8, 0)]
-    right = pl.pallas_call(
+    right, pair, last = pl.pallas_call(
         pick_kernel,
-        out_shape=jax.ShapeDtypeStruct((3, row_count, PIECE), jnp.bfloat16),
+        out_shape=[
+            jax.ShapeDtypeStruct((3, row_count, PIECE), jnp.bfloat16),
+            jax.ShapeDtypeStruct((2, row_count, PIECE), jnp.bfloat16),
+            jax.ShapeDtypeStruct((row_count, PIECE), jnp.bfloat16),
+        ],
         in_specs=[smem] + [anywhere] * len(sources),
-        out_specs=vmem,
-        scratch_shapes=[pltpu.SemaphoreType.DMA((SLOTS,))],
+        out_specs=[vmem] * 3,
+        scratch_shapes=[pltpu.SemaphoreType.DMA((2 * SLOTS,))],
         compiler_params=pltpu.CompilerParams(vmem_limit_bytes=16 * 2**20),
     )(table, *sources)
-    right_y = lax.ppermute(right[:2], "yl", swap)
-    last_y = lax.ppermute(right[2], ("yl", "z"), swap_first)
+    right_y = lax.ppermute(pair, "yl", swap)
+    last_y = lax.ppermute(last, ("yl", "z"), swap_first)
     right_c = lax.ppermute(right, "co", swap)
     right_yc = lax.ppermute(right_y, "co", swap)
     last_yc = lax.ppermute(last_y, ("co", "z"), swap_first)
@@ -220,9 +233,11 @@
         lambda *refs: tile_kernel(row_count - 1, *refs),
         out_shape=jax.ShapeDtypeStruct((SLOTS, PIECE, BLK), jnp.bfloat16),
         in_specs=[smem] + [anywhere] * len(sources) + [vmem] * 6,
-        out_specs=vmem,
+        out_specs=anywhere,
         scratch_shapes=[
             pltpu.VMEM((SLOTS, row_count, PIECE), jnp.bfloat16),
+            pltpu.VMEM((SLOTS, PIECE, BLK), jnp.bfloat16),
+            pltpu.SemaphoreType.DMA((SLOTS,)),
             pltpu.SemaphoreType.DMA((SLOTS,)),
         ],
         compiler_params=pltpu.CompilerParams(vmem_limit_bytes=32 * 2**20),

time: 92.5 us -> 91.2 us (0.986)
  waiting for transfers between devices: 15.8 us -> 11 us
  starting transfers between devices: 56.6 us -> 60.3 us
  local copies, waits for them, and re-layouts: 3.01 us -> 1.41 us
    ppermute x1, starting transfers between devices: 4.66 us -> 7.63 us  [shards(): last_yc = lax.ppermute(last_y, ('co', 'z'), swap_first)]
    ppermute x2, waiting for transfers between devices: 6.91 us -> 3.99 us  [the longest x1 3.99 us: shards(): last_y = lax.ppermute(last, ('yl', 'z'), swap_first)]
    ppermute x6, waiting for transfers between devices: 8.66 us -> 6.78 us  [shards(): arrived = [lax.ppermute(centered, EVERY, pairs) for pairs in rounds]]
    pallas_call x1, Pallas kernels: 1.02 us -> 2.05 us  [shards(): pl.pallas_call(pick_kernel, out_shape=[jax.ShapeDtypeStruct((3, row_count...]
  transfers between devices with their start and end apart: 14 -> 14, of which waited for: 3 -> 3; matrix products, arithmetic and copies ran while one was open for 7% -> 6% of each run, Pallas kernels for 1% -> 2%
where the time goes in v2:
time: 91.2 us; the launch traced here: 90 us
  starting transfers between devices  60.3 us (66%)
  waiting for transfers between devices  11 us (12%)
  blocking collectives  6.51 us (7%)
  Pallas kernels  5.89 us (6%)
  matrix products  2.79 us (3%)
  local copies, waits for them, and re-layouts  1.41 us (2%)
  other arithmetic  1.28 us (1%)
    ppermute x6, starting transfers between devices, shards(): arrived = [lax.ppermute(centered, EVERY, pairs) for pairs in rounds]  21.7 us
    all_to_all x1, starting transfers between devices, shards(): lax.all_to_all(jnp.broadcast_to(part, (8, *part.shape)), 'z', 0, 0)  9.97 us
    all_to_all x1, starting transfers between devices, shards(): lax.all_to_all(gram.reshape(8, -1, row_count), ('x', 'yh'), 0, 0).sum(0)  8.6 us
    ppermute x1, starting transfers between devices, shards(): last_yc = lax.ppermute(last_y, ('co', 'z'), swap_first)  7.63 us
    ppermute x6, waiting for transfers between devices, shards(): arrived = [lax.ppermute(centered, EVERY, pairs) for pairs in rounds]  6.78 us
    all_gather x1, blocking collectives, shards(): lax.all_gather(embedding, BATCH, axis=0, tiled=True).astype(jnp.float32)  6.51 us
    ppermute x1, starting transfers between devices, shards(): right_c = lax.ppermute(right, 'co', swap)  4.61 us
    all_to_all x1, starting transfers between devices, shards(): lax.all_to_all(jnp.broadcast_to(part, (8, *part.shape)), ('x', 'yh'), 0, 0)  4.24 us
  transfers between devices with their start and end apart: 14, of which 3 were waited for; matrix products, arithmetic and copies ran while one was open for 6% of the time, Pallas kernels for 2%

profile of v2, /device:TPU:25, one launch (start us, length us, event | category | flops | bytes accessed | tf_op | source)
XLA Modules:
  0.0 90.0 jit_solution(8489360524382398634)
XLA Ops:
  0.6 6.5 %all_gather.3 = bf16[512,256]{1,0:T(8,128)(2,1)S(1)} all-gather(bf16[128,256]{1,0:T(8,128)(2,1)} %param.2), channel_id=1, replica_groups=mesh['yl'=2,'co'=2,'z'=8,'x'=4,'yh'=2] {'yl','co'}, dimensions={0}, use_global_device_ids=true | all-gather | bytes 327680 | tf_op jit(solution)/shard_map/all_gather | solution.py:182
  7.4 4.4 %collective-permute-start = (bf16[512,256]{1,0:T(8,128)(2,1)S(1)}, bf16[512,256]{1,0:T(8,128)(2,1)S(1)}, u32[]{:S(2)}, u32[]{:S(2)}) collective-permute-start(bf16[512,256]{1,0:T(8,128)(2,1)S(1)} %get-tuple-element.10.refs_6_.refs_7_), channel_id=1, source_target_pairs={{0,4},{1,75},{2,133},{3,206},{4,30},{5,65},{6,155},{7,218},{8,36},... | collective-permute-start | bytes 786440 | tf_op jit(solution)/shard_map/ppermute | solution.py:188
  11.8 1.8 %fusion.13 = f32[128,512]{1,0:T(8,128)} fusion(bf16[512,256]{1,0:T(8,128)(2,1)S(1)} %get-tuple-element.10.refs_6_.refs_7_, bf16[128,256]{1,0:T(8,128)(2,1)} %param.2, f32[256]{0:T(256)S(1)} %broadcast_multiply_fusion), kind=kOutput, calls=%fused_computation.20 | convolution fusion | flops 33685504 | bytes 590848 | tf_op jit(solution)/shard_map/dot_general | solution.py:194
  13.5 8.6 %all-to-all-start = ((f32[8,16,512]{2,1,0:T(8,128)}), f32[8,16,512]{2,1,0:T(8,128)S(1)}, u32[]{:S(2)}, u32[]{:S(2)}) async-start(f32[8,16,512]{2,1,0:T(8,128)} %bitcast), calls=%async_computation | async-start | bytes 524288 | tf_op jit(solution)/shard_map/all_to_all | solution.py:197
  22.1 4.4 %collective-permute-start.1 = (bf16[512,256]{1,0:T(8,128)(2,1)S(1)}, bf16[512,256]{1,0:T(8,128)(2,1)S(1)}, u32[]{:S(2)}, u32[]{:S(2)}) collective-permute-start(bf16[512,256]{1,0:T(8,128)(2,1)S(1)} %get-tuple-element.10.refs_6_.refs_7_), channel_id=1, source_target_pairs={{0,8},{1,67},{2,141},{3,194},{4,26},{5,83},{6,151},{7,214},{8,32},... | collective-permute-start | bytes 786440 | tf_op jit(solution)/shard_map/ppermute | solution.py:188
  26.5 5.1 %collective-permute-start.2 = (bf16[512,256]{1,0:T(8,128)(2,1)S(1)}, bf16[512,256]{1,0:T(8,128)(2,1)S(1)}, u32[]{:S(2)}, u32[]{:S(2)}) collective-permute-start(bf16[512,256]{1,0:T(8,128)(2,1)S(1)} %get-tuple-element.10.refs_6_.refs_7_), channel_id=1, source_target_pairs={{0,12},{1,79},{2,137},{3,198},{4,18},{5,91},{6,129},{7,222},{8,40}... | collective-permute-start | bytes 786440 | tf_op jit(solution)/shard_map/ppermute | solution.py:188
  31.6 5.3 %collective-permute-start.3 = (bf16[512,256]{1,0:T(8,128)(2,1)S(1)}, bf16[512,256]{1,0:T(8,128)(2,1)S(1)}, u32[]{:S(2)}, u32[]{:S(2)}) collective-permute-start(bf16[512,256]{1,0:T(8,128)(2,1)S(1)} %get-tuple-element.10.refs_6_.refs_7_), channel_id=1, source_target_pairs={{2,129},{3,202},{4,22},{5,87},{6,147},{7,210},{8,44},{9,105},{10,1... | collective-permute-start | bytes 786440 | tf_op jit(solution)/shard_map/ppermute | solution.py:188
  36.9 1.3 %collective-permute-start.4 = (bf16[512,256]{1,0:T(8,128)(2,1)S(1)}, bf16[512,256]{1,0:T(8,128)(2,1)S(1)}, u32[]{:S(2)}, u32[]{:S(2)}) collective-permute-start(bf16[512,256]{1,0:T(8,128)(2,1)S(1)} %get-tuple-element.10.refs_6_.refs_7_), channel_id=1, source_target_pairs={{1,71},{26,135},{46,129},{48,2},{49,65},{51,194},{52,4},{53,67},{5... | collective-permute-start | bytes 786440 | tf_op jit(solution)/shard_map/ppermute | solution.py:188
  38.2 1.3 %collective-permute-start.5 = (bf16[512,256]{1,0:T(8,128)(2,1)S(1)}, bf16[512,256]{1,0:T(8,128)(2,1)S(1)}, u32[]{:S(2)}, u32[]{:S(2)}) collective-permute-start(bf16[512,256]{1,0:T(8,128)(2,1)S(1)} %get-tuple-element.10.refs_6_.refs_7_), channel_id=1, source_target_pairs={{50,129},{176,1},{179,193}} | collective-permute-start | bytes 786440 | tf_op jit(solution)/shard_map/ppermute | solution.py:188
  39.5 0.7 broadcast_in_dim.18
  40.2 10.0 %all-to-all-start.1 = ((bf16[8,16,512]{2,1,0:T(8,128)(2,1)}), bf16[8,16,512]{2,1,0:T(8,128)(2,1)S(1)}, u32[]{:S(2)}, u32[]{:S(2)}) async-start(bf16[8,16,512]{2,1,0:T(8,128)(2,1)} %broadcast_in_dim.18), calls=%async_computation.1 | async-start | bytes 262144 | tf_op jit(solution)/shard_map/all_to_all | solution.py:199
  50.2 6.8 %collective-permute-done.4.refs_4_.refs_5_ = bf16[512,256]{1,0:T(8,128)(2,1)S(1)} collective-permute-done((bf16[512,256]{1,0:T(8,128)(2,1)S(1)}, bf16[512,256]{1,0:T(8,128)(2,1)S(1)}, u32[]{:S(2)}, u32[]{:S(2)}) %collective-permute-start.4) | collective-permute-done | bytes 262176 | tf_op jit(solution)/shard_map/ppermute | solution.py:188
  57.0 2.1 %shard_map.41 = (bf16[3,512,256]{2,1,0:T(8,128)(2,1)S(1)}, bf16[2,512,256]{2,1,0:T(8,128)(2,1)}, bf16[512,256]{1,0:T(8,128)(2,1)}) custom-call(s32[4096]{0:T(1024)S(1)} %copy-done, bf16[512,256]{1,0:T(8,128)(2,1)S(1)} %collective-permute-done.refs_0_.refs_1_, bf16[512,256]{1,0:T(8,128)(2,1)S(1)} %collective-permute-done.1.refs_1_.refs_2_, ...), custom_call_target="tpu_custom_call" | custom-call | tf_op jit(solution)/shard_map/pallas_call | solution.py:215
  59.2 3.3 %collective-permute-start.9 = (bf16[512,256]{1,0:T(8,128)(2,1)}, bf16[512,256]{1,0:T(8,128)(2,1)}, u32[]{:S(2)}, u32[]{:S(2)}) collective-permute-start(bf16[512,256]{1,0:T(8,128)(2,1)} %get-tuple-element.7), channel_id=1, source_target_pairs={{0,128},{128,0},{1,129},{129,1},{2,130},{130,2},{3,131},{131,3},{4... | collective-permute-start | bytes 786440 | tf_op jit(solution)/shard_map/ppermute | solution.py:228
  62.6 0.7 broadcast_in_dim.19
  63.3 4.2 %all-to-all-start.2 = ((f32[8,16,512]{2,1,0:T(8,128)}), f32[8,16,512]{2,1,0:T(8,128)}, u32[]{:S(2)}, u32[]{:S(2)}) async-start(f32[8,16,512]{2,1,0:T(8,128)} %broadcast_in_dim.19), calls=%async_computation.2 | async-start | bytes 524288 | tf_op jit(solution)/shard_map/all_to_all | solution.py:200
  67.5 4.6 %collective-permute-start.6 = (bf16[3,512,256]{2,1,0:T(8,128)(2,1)S(1)}, bf16[3,512,256]{2,1,0:T(8,128)(2,1)S(1)}, u32[]{:S(2)}, u32[]{:S(2)}) collective-permute-start(bf16[3,512,256]{2,1,0:T(8,128)(2,1)S(1)} %get-tuple-element.5.refs_8_), channel_id=1, source_target_pairs={{0,64},{64,0},{1,65},{65,1},{2,66},{66,2},{3,67},{67,3},{4,68},{68... | collective-permute-start | bytes 2359304 | tf_op jit(solution)/shard_map/ppermute | solution.py:229
  72.2 4.0 %collective-permute-done.9.refs_12_ = bf16[512,256]{1,0:T(8,128)(2,1)} collective-permute-done((bf16[512,256]{1,0:T(8,128)(2,1)}, bf16[512,256]{1,0:T(8,128)(2,1)}, u32[]{:S(2)}, u32[]{:S(2)}) %collective-permute-start.9) | collective-permute-done | bytes 262176 | tf_op jit(solution)/shard_map/ppermute | solution.py:228
  76.1 7.6 %collective-permute-start.10 = (bf16[512,256]{1,0:T(8,128)(2,1)}, bf16[512,256]{1,0:T(8,128)(2,1)}, u32[]{:S(2)}, u32[]{:S(2)}) collective-permute-start(bf16[512,256]{1,0:T(8,128)(2,1)} %collective-permute-done.9.refs_12_), channel_id=1, source_target_pairs={{0,64},{64,0},{1,65},{65,1},{2,66},{66,2},{3,67},{67,3},{4,68},{68... | collective-permute-start | bytes 786440 | tf_op jit(solution)/shard_map/ppermute | solution.py:231
  83.9 1.0 %fusion.10 = (bf16[128,512]{1,0:T(8,128)(2,1)S(1)}, bf16[128,512]{1,0:T(8,128)(2,1)S(1)}) fusion(f32[8,16,512]{2,1,0:T(8,128)} %all-to-all-done.2), kind=kLoop, calls=%fused_computation.15 | loop fusion | flops 262144 | bytes 524288 | tf_op jit(solution)/shard_map/convert_element_type | solution.py:202
  84.9 0.2 fusion.16
  85.1 0.8 fusion.3
  85.9 0.2 collective-permute-done.8.refs_11_
  86.1 3.8 %shard_map.42 = bf16[3,256,1024]{2,1,0:T(8,128)(2,1)} custom-call(s32[4096]{0:T(1024)S(1)} %copy-done, bf16[512,256]{1,0:T(8,128)(2,1)S(1)} %collective-permute-done.refs_0_.refs_1_, bf16[512,256]{1,0:T(8,128)(2,1)S(1)} %collective-permute-done.1.refs_1_.refs_2_, bf16[512,256]{1,0:T(8,128)(2,1)S(1)} %collective-permute-done.2.refs_2_.refs_3_, ...), custom_call_target="tpu_custom_call" | custom-call | tf_op jit(solution)/shard_map/pallas_call | solution.py:232
  (24 shorter events, 0.5 us)
Async XLA Ops:
  0.6 56.4 %copy-start = (s32[4096]{0:T(1024)S(1)}, s32[4096]{0:T(1024)}, u32[]{:S(2)}) copy-start(s32[4096]{0:T(1024)} %constant.18.clone.table_ref.refs_0_) | copy-start | bytes 49156
  7.4 30.8 %collective-permute-start = (bf16[512,256]{1,0:T(8,128)(2,1)S(1)}, bf16[512,256]{1,0:T(8,128)(2,1)S(1)}, u32[]{:S(2)}, u32[]{:S(2)}) collective-permute-start(bf16[512,256]{1,0:T(8,128)(2,1)S(1)} %get-tuple-element.10.refs_6_.refs_7_), channel_id=1, source_target_pairs={{0,4},{1,75},{2,133},{3,206},{4,30},{5,65},{6,155},{7,218},{8,36},... | collective-permute-start | bytes 786440 | tf_op jit(solution)/shard_map/ppermute | solution.py:188
  13.5 26.0 %all-to-all-start = ((f32[8,16,512]{2,1,0:T(8,128)}), f32[8,16,512]{2,1,0:T(8,128)S(1)}, u32[]{:S(2)}, u32[]{:S(2)}) async-start(f32[8,16,512]{2,1,0:T(8,128)} %bitcast), calls=%async_computation | async-start | bytes 524288 | tf_op jit(solution)/shard_map/all_to_all | solution.py:197
  22.1 28.1 %collective-permute-start.1 = (bf16[512,256]{1,0:T(8,128)(2,1)S(1)}, bf16[512,256]{1,0:T(8,128)(2,1)S(1)}, u32[]{:S(2)}, u32[]{:S(2)}) collective-permute-start(bf16[512,256]{1,0:T(8,128)(2,1)S(1)} %get-tuple-element.10.refs_6_.refs_7_), channel_id=1, source_target_pairs={{0,8},{1,67},{2,141},{3,194},{4,26},{5,83},{6,151},{7,214},{8,32},... | collective-permute-start | bytes 786440 | tf_op jit(solution)/shard_map/ppermute | solution.py:188
  26.5 23.7 %collective-permute-start.2 = (bf16[512,256]{1,0:T(8,128)(2,1)S(1)}, bf16[512,256]{1,0:T(8,128)(2,1)S(1)}, u32[]{:S(2)}, u32[]{:S(2)}) collective-permute-start(bf16[512,256]{1,0:T(8,128)(2,1)S(1)} %get-tuple-element.10.refs_6_.refs_7_), channel_id=1, source_target_pairs={{0,12},{1,79},{2,137},{3,198},{4,18},{5,91},{6,129},{7,222},{8,40}... | collective-permute-start | bytes 786440 | tf_op jit(solution)/shard_map/ppermute | solution.py:188
  31.6 18.6 %collective-permute-start.3 = (bf16[512,256]{1,0:T(8,128)(2,1)S(1)}, bf16[512,256]{1,0:T(8,128)(2,1)S(1)}, u32[]{:S(2)}, u32[]{:S(2)}) collective-permute-start(bf16[512,256]{1,0:T(8,128)(2,1)S(1)} %get-tuple-element.10.refs_6_.refs_7_), channel_id=1, source_target_pairs={{2,129},{3,202},{4,22},{5,87},{6,147},{7,210},{8,44},{9,105},{10,1... | collective-permute-start | bytes 786440 | tf_op jit(solution)/shard_map/ppermute | solution.py:188
  36.9 20.1 %collective-permute-start.4 = (bf16[512,256]{1,0:T(8,128)(2,1)S(1)}, bf16[512,256]{1,0:T(8,128)(2,1)S(1)}, u32[]{:S(2)}, u32[]{:S(2)}) collective-permute-start(bf16[512,256]{1,0:T(8,128)(2,1)S(1)} %get-tuple-element.10.refs_6_.refs_7_), channel_id=1, source_target_pairs={{1,71},{26,135},{46,129},{48,2},{49,65},{51,194},{52,4},{53,67},{5... | collective-permute-start | bytes 786440 | tf_op jit(solution)/shard_map/ppermute | solution.py:188
  38.2 18.8 %collective-permute-start.5 = (bf16[512,256]{1,0:T(8,128)(2,1)S(1)}, bf16[512,256]{1,0:T(8,128)(2,1)S(1)}, u32[]{:S(2)}, u32[]{:S(2)}) collective-permute-start(bf16[512,256]{1,0:T(8,128)(2,1)S(1)} %get-tuple-element.10.refs_6_.refs_7_), channel_id=1, source_target_pairs={{50,129},{176,1},{179,193}} | collective-permute-start | bytes 786440 | tf_op jit(solution)/shard_map/ppermute | solution.py:188
  40.2 22.3 %all-to-all-start.1 = ((bf16[8,16,512]{2,1,0:T(8,128)(2,1)}), bf16[8,16,512]{2,1,0:T(8,128)(2,1)S(1)}, u32[]{:S(2)}, u32[]{:S(2)}) async-start(bf16[8,16,512]{2,1,0:T(8,128)(2,1)} %broadcast_in_dim.18), calls=%async_computation.1 | async-start | bytes 262144 | tf_op jit(solution)/shard_map/all_to_all | solution.py:199
  50.2 34.9 %copy-start.1 = (bf16[128,256]{1,0:T(8,128)(2,1)S(1)}, bf16[128,256]{1,0:T(8,128)(2,1)}, u32[]{:S(2)}) copy-start(bf16[128,256]{1,0:T(8,128)(2,1)} %param.2) | copy-start | bytes 196612
  59.1 24.7 %collective-permute-start.7 = (bf16[2,512,256]{2,1,0:T(8,128)(2,1)}, bf16[2,512,256]{2,1,0:T(8,128)(2,1)}, u32[]{:S(2)}, u32[]{:S(2)}) collective-permute-start(bf16[2,512,256]{2,1,0:T(8,128)(2,1)} %get-tuple-element.6), channel_id=1, source_target_pairs={{0,128},{128,0},{1,129},{129,1},{2,130},{130,2},{3,131},{131,3},{4... | collective-permute-start | bytes 1572872 | tf_op jit(solution)/shard_map/ppermute | solution.py:227
  59.2 17.0 %collective-permute-start.9 = (bf16[512,256]{1,0:T(8,128)(2,1)}, bf16[512,256]{1,0:T(8,128)(2,1)}, u32[]{:S(2)}, u32[]{:S(2)}) collective-permute-start(bf16[512,256]{1,0:T(8,128)(2,1)} %get-tuple-element.7), channel_id=1, source_target_pairs={{0,128},{128,0},{1,129},{129,1},{2,130},{130,2},{3,131},{131,3},{4... | collective-permute-start | bytes 786440 | tf_op jit(solution)/shard_map/ppermute | solution.py:228
  63.3 20.6 %all-to-all-start.2 = ((f32[8,16,512]{2,1,0:T(8,128)}), f32[8,16,512]{2,1,0:T(8,128)}, u32[]{:S(2)}, u32[]{:S(2)}) async-start(f32[8,16,512]{2,1,0:T(8,128)} %broadcast_in_dim.19), calls=%async_computation.2 | async-start | bytes 524288 | tf_op jit(solution)/shard_map/all_to_all | solution.py:200
  67.5 18.4 %collective-permute-start.6 = (bf16[3,512,256]{2,1,0:T(8,128)(2,1)S(1)}, bf16[3,512,256]{2,1,0:T(8,128)(2,1)S(1)}, u32[]{:S(2)}, u32[]{:S(2)}) collective-permute-start(bf16[3,512,256]{2,1,0:T(8,128)(2,1)S(1)} %get-tuple-element.5.refs_8_), channel_id=1, source_target_pairs={{0,64},{64,0},{1,65},{65,1},{2,66},{66,2},{3,67},{67,3},{4,68},{68... | collective-permute-start | bytes 2359304 | tf_op jit(solution)/shard_map/ppermute | solution.py:229
  76.1 9.8 %collective-permute-start.10 = (bf16[512,256]{1,0:T(8,128)(2,1)}, bf16[512,256]{1,0:T(8,128)(2,1)}, u32[]{:S(2)}, u32[]{:S(2)}) collective-permute-start(bf16[512,256]{1,0:T(8,128)(2,1)} %collective-permute-done.9.refs_12_), channel_id=1, source_target_pairs={{0,64},{64,0},{1,65},{65,1},{2,66},{66,2},{3,67},{67,3},{4,68},{68... | collective-permute-start | bytes 786440 | tf_op jit(solution)/shard_map/ppermute | solution.py:231
  83.8 2.3 %collective-permute-start.8 = (bf16[2,512,256]{2,1,0:T(8,128)(2,1)}, bf16[2,512,256]{2,1,0:T(8,128)(2,1)}, u32[]{:S(2)}, u32[]{:S(2)}) collective-permute-start(bf16[2,512,256]{2,1,0:T(8,128)(2,1)} %collective-permute-done.7.refs_10_), channel_id=1, source_target_pairs={{0,64},{64,0},{1,65},{65,1},{2,66},{66,2},{3,67},{67,3},{4,68},{68... | collective-permute-start | bytes 1572872 | tf_op jit(solution)/shard_map/ppermute | solution.py:230
